TPU v7x, 128 devices: a whole 4x4x4 slice. The times are simulated.
128 devices in a mesh: row: 8 (over x, core), col: 16 (over y, z).
Axes of the slice: x: 4, y: 4, z: 4, core: 2. Of those that a mesh axis runs over, the one named last changes fastest.
Arguments:
- left_h: float32 [16384, 512], P('row', 'col'), may hold values from 0 to 3.0517578e-05
- left_l: float32 [16384, 512], P('row', 'col'), may hold values from 0 to 3.0517578e-05
- right_h: float32 [512, 16384], P('row', 'col'), may hold values from 0 to 3.0517578e-05
- right_l: float32 [512, 16384], P('row', 'col'), may hold values from 0 to 3.0517578e-05
Outputs:
- cross_sum: float32 [16384, 16384], P('row', 'col')
- square_h: float32 [16384, 16384], P('row', 'col')
- square_l: float32 [16384, 16384], P('row', 'col')
All inputs are finite; a program needn't handle non-finite values.
Results may differ from a plain program's by a relative error of at most 0.00005.
Values sent between devices are 32-bit elements; how exact they have to be, the bound alone decides.
A program may use at most 128 MiB of HBM per device.

v0:
```python
import jax
import jax.numpy as jnp
from jax import lax
from jax.sharding import PartitionSpec as P

KW = 512


def product(left, right):
    return jnp.dot(left, right, preferred_element_type=jnp.float32, precision=lax.Precision.HIGHEST)


def accumulate(part_h, part_l, rows_h, rows_l):
    cross_sum = product(part_h, rows_l) + product(part_l, rows_h)
    square_h = product(part_h, rows_h)
    square_l = product(part_l, rows_l)
    return (cross_sum, square_h, square_l)


def per_device(left_h, left_l, right_h, right_l):
    whole_h, whole_l = (
        lax.all_gather(left_h, "col", axis=1, tiled=True),
        lax.all_gather(left_l, "col", axis=1, tiled=True),
    )
    result = accumulate(
        whole_h,
        whole_l,
        lax.all_gather(right_h, "row", axis=0, tiled=True),
        lax.all_gather(right_l, "row", axis=0, tiled=True),
    )
    factor = 2.0**30 / KW
    return (factor * result[0], factor * result[1], factor * result[2])


def solution(mesh):
    in_specs = (P("row", "col"), P("row", "col"), P("row", "col"), P("row", "col"))
    out_specs = (P("row", "col"), P("row", "col"), P("row", "col"))
    return jax.shard_map(
        per_device, mesh=mesh, in_specs=in_specs, out_specs=out_specs, check_vma=False
    )
```

profile of v0, /device:TPU:0, one launch (start us, length us, event | category | flops | bytes accessed | tf_op | source)
XLA Modules:
  0.0 212.0 jit_solution(18160205850447754203)
XLA Ops:
  7.2 0.0 all-gather.7.cloned.1.call-start
  7.2 0.7 all-gather.7.cloned.1.call-update
  7.9 0.0 all-gather.9.cloned.1.call-start
  7.9 0.7 all-gather.9.cloned.1.call-update
  8.6 0.0 all-gather.5.cloned.1.call-start
  8.7 0.7 all-gather.5.cloned.1.call-update
  9.4 0.0 all-gather.11.cloned.1.call-start
  9.4 0.5 all-gather.11.cloned.1.call-update
  10.0 27.4 %all-gather.7.cloned.1.call-done = f32[512,1024]{1,0:T(8,128)} async-done(((f32[64,1024]{1,0:T(8,128)}), f32[512,1024]{1,0:T(8,128)}) %all-gather.7.cloned.1.call-update) | async-done | bytes 2097168 | tf_op jit(solution)/shard_map/all_gather | solution.py:29
  37.3 0.0 copy-start.2
  37.3 54.1 %all-gather.9.cloned.1.call-done = f32[2048,512]{0,1:T(8,128)} async-done(((f32[2048,32]{0,1:T(8,128)}), f32[2048,512]{0,1:T(8,128)}) %all-gather.9.cloned.1.call-update) | async-done | bytes 4194320 | tf_op jit(solution)/shard_map/all_gather | solution.py:23
  91.5 17.9 %convolution_multiply_fusion = f32[2048,1024]{1,0:T(8,128)} fusion(f32[2048,512]{0,1:T(8,128)} %all-gather.9.cloned.1.call-done, f32[512,1024]{1,0:T(8,128)} %all-gather.7.cloned.1.call-done), kind=kOutput, calls=%fused_computation.1 | convolution fusion | flops 12886999040 | bytes 14680064 | tf_op jit(solution)/shard_map/dot_general | solution.py:10
  109.4 35.6 %all-gather.5.cloned.1.call-done = f32[2048,512]{0,1:T(8,128)} async-done(((f32[2048,32]{0,1:T(8,128)}), f32[2048,512]{0,1:T(8,128)}) %all-gather.5.cloned.1.call-update) | async-done | bytes 4194320 | tf_op jit(solution)/shard_map/all_gather | solution.py:22
  144.9 0.0 copy-done.2
  144.9 17.2 %fusion = f32[2048,1024]{1,0:T(8,128)} fusion(f32[2048,512]{0,1:T(8,128)} %all-gather.5.cloned.1.call-done, f32[512,1024]{1,0:T(8,128)S(1)} %copy-done.2), kind=kOutput, calls=%fused_computation.3 | convolution fusion | flops 12884901888 | bytes 14680064 | tf_op jit(solution)/shard_map/dot_general | solution.py:10
  162.1 9.1 %all-gather.11.cloned.1.call-done = f32[512,1024]{1,0:T(8,128)} async-done(((f32[64,1024]{1,0:T(8,128)}), f32[512,1024]{1,0:T(8,128)}) %all-gather.11.cloned.1.call-update) | async-done | bytes 2097168 | tf_op jit(solution)/shard_map/all_gather | solution.py:28
  171.2 0.0 copy-start
  171.2 0.0 copy-start.1
  171.2 0.0 copy-start.3
  171.2 18.2 %convolution_multiply_fusion.1 = f32[2048,1024]{1,0:T(8,128)} fusion(f32[2048,512]{0,1:T(8,128)} %all-gather.5.cloned.1.call-done, f32[512,1024]{1,0:T(8,128)} %all-gather.11.cloned.1.call-done), kind=kOutput, calls=%fused_computation.2 | convolution fusion | flops 12886999040 | bytes 14680064 | tf_op jit(solution)/shard_map/dot_general | solution.py:10
  189.5 0.0 copy-done
  189.5 0.0 copy-done.1
  189.5 0.0 copy-done.3
  189.5 16.0 %add_multiply_fusion = f32[2048,1024]{1,0:T(8,128)} fusion(f32[2048,1024]{1,0:T(8,128)S(1)} %copy-done, f32[2048,512]{0,1:T(8,128)S(1)} %copy-done.1, f32[512,1024]{1,0:T(8,128)S(1)} %copy-done.3), kind=kOutput, calls=%fused_computation | convolution fusion | flops 12889096192 | bytes 23068672 | tf_op jit(solution)/shard_map/dot_general | solution.py:10
Async XLA Ops:
  7.2 30.2 %all-gather.7.cloned.1.call-start = ((), (), s32[]{:S(2)}) async-start(), calls=%async_computation.1 | async-start | bytes 2359296 | tf_op jit(solution)/shard_map/all_gather | solution.py:29
  7.9 83.6 %all-gather.9.cloned.1.call-start = ((), (), s32[]{:S(2)}) async-start(), calls=%async_computation.2 | async-start | bytes 4456448 | tf_op jit(solution)/shard_map/all_gather | solution.py:23
  8.6 136.3 %all-gather.5.cloned.1.call-start = ((), (), s32[]{:S(2)}) async-start(), calls=%async_computation | async-start | bytes 4456448 | tf_op jit(solution)/shard_map/all_gather | solution.py:22
  9.4 161.8 %all-gather.11.cloned.1.call-start = ((), (), s32[]{:S(2)}) async-start(), calls=%async_computation.3 | async-start | bytes 2359296 | tf_op jit(solution)/shard_map/all_gather | solution.py:28
  37.3 107.6 %copy-start.2 = (f32[512,1024]{1,0:T(8,128)S(1)}, f32[512,1024]{1,0:T(8,128)}, u32[]{:S(2)}) copy-start(f32[512,1024]{1,0:T(8,128)} %all-gather.7.cloned.1.call-done) | copy-start | bytes 6291460
  171.2 18.3 %copy-start = (f32[2048,1024]{1,0:T(8,128)S(1)}, f32[2048,1024]{1,0:T(8,128)}, u32[]{:S(2)}) copy-start(f32[2048,1024]{1,0:T(8,128)} %fusion) | copy-start | bytes 25165828
  171.2 18.3 %copy-start.1 = (f32[2048,512]{0,1:T(8,128)S(1)}, f32[2048,512]{0,1:T(8,128)}, u32[]{:S(2)}) copy-start(f32[2048,512]{0,1:T(8,128)} %all-gather.9.cloned.1.call-done) | copy-start | bytes 12582916
  171.2 18.3 %copy-start.3 = (f32[512,1024]{1,0:T(8,128)S(1)}, f32[512,1024]{1,0:T(8,128)}, u32[]{:S(2)}) copy-start(f32[512,1024]{1,0:T(8,128)} %all-gather.11.cloned.1.call-done) | copy-start | bytes 6291460
Sparse Core Ops, SparseCore 0:
  9.7 27.5 all-gather.6
  39.5 51.9 all-gather.8
  93.6 51.2 all-gather.4
  146.5 24.6 all-gather.10
where the time goes:
time: 213 us; the launch traced here: 212 us
  waiting for transfers between devices  129 us (61%)
  matrix products  69.3 us (33%)
  between operations  13.8 us (6%)
    dot_general x4, matrix products, product(): jnp.dot(left, right, preferred_element_type=jnp.float32, precision=lax.Pr...  69.3 us
    all_gather x1, waiting for transfers between devices, per_device(): lax.all_gather(left_l, 'col', axis=1, tiled=True)  54.1 us
    all_gather x1, waiting for transfers between devices, per_device(): lax.all_gather(left_h, 'col', axis=1, tiled=True)  35.6 us
    all_gather x1, waiting for transfers between devices, per_device(): lax.all_gather(right_l, 'row', axis=0, tiled=True)  27.4 us
    all_gather x1, waiting for transfers between devices, per_device(): lax.all_gather(right_h, 'row', axis=0, tiled=True)  9.13 us
  transfers between devices with their start and end apart: 4, of which 4 were waited for; matrix products, arithmetic and copies ran while one was open for 17% of the time, Pallas kernels for 0%

commit v1 on v0

v1 whole, which is shorter than its diff:
```python
import functools

import jax
import jax.numpy as jnp
from jax import lax
from jax.experimental import pallas as pl
from jax.experimental.pallas import tpu as pltpu
from jax.sharding import PartitionSpec as P

KW = 512
SCALE = 2.0**30 / KW
MESH = pl.DeviceIdType.MESH
F32, BF16 = jnp.float32, jnp.bfloat16

M, N, KD, RD = 2048, 1024, 32, 64
CH = 512
NCH = M // CH
EARLY = NCH - 1
SUB = CH // 4

dot = functools.partial(jnp.dot, preferred_element_type=F32)


def split(value):
    high = value.astype(BF16)
    return high, (value - high.astype(F32)).astype(BF16)


def times_hh(a, b, rows):
    return SCALE * (dot(a[rows, 0:1024], b[1024:2048, :]) + dot(a[rows, 512:1024], b[1024:1536, :]))


def times_ll(a, b, rows):
    return SCALE * (dot(a[rows, 1024:2048], b[0:1024, :]) + dot(a[rows, 1536:2048], b[0:512, :]))


def times_cross(a, b, rows):
    small = dot(a[rows, :], b[:, :])
    return SCALE * (small + (dot(a[rows, 512:1024], b[0:512, :]) + dot(a[rows, 1536:2048], b[1024:1536, :])))


def gather_kernel(
    lth, ltl, rth, rtl,
    out_c, out_h, out_l, a_last, b,
    lt, rl, rr, a, load_sem,
    s1s, s1r, s2s, s2r, s3s, s3r, s4s, s4r, rs, rv,
):
    row, col = lax.axis_index("row"), lax.axis_index("col")
    x, core, y, z = row // 2, row % 2, col // 4, col % 4

    def wrap(v):
        return lax.rem(v + 8, 4)

    def at(dx=0, dc=0, dy=0, dz=0):
        new_core = 1 - core if dc else core
        return (wrap(x + dx) * 2 + new_core, wrap(y + dy) * 4 + wrap(z + dz))

    step = (1, -1)
    yz = tuple(tuple(at(dy=d) if ax == 0 else at(dz=d) for d in step) for ax in (0, 1))
    xs = tuple(at(dx=d) for d in step)
    twin = at(dc=1)

    loads = [pltpu.make_async_copy(ref, lt.at[i], load_sem.at[i]) for i, ref in enumerate((lth, ltl))]
    own_right = [pltpu.make_async_copy(ref, rr.at[i, row], load_sem.at[2 + i]) for i, ref in enumerate((rth, rtl))]
    for copy in loads + own_right:
        copy.start()
    barrier = pltpu.get_barrier_semaphore()
    for device in (*yz[0], *yz[1], *xs, twin):
        pl.semaphore_signal(barrier, 1, device_id=device, device_id_type=MESH)
    for copy in loads:
        copy.wait()

    for c in range(NCH):
        for arr in (0, 1):
            parts = []
            for p in range(4):
                start = pl.multiple_of(c * CH + wrap(p - z) * SUB, SUB)
                parts.append(lt[arr, :, pl.ds(start, SUB)])
            rl[arr, y, z, c] = jnp.concatenate(parts, axis=0).T

    pl.semaphore_wait(barrier, 7)
    started = []

    def send(src, dst, send_sem, recv_sem, device):
        copy = pltpu.make_async_remote_copy(
            src_ref=src, dst_ref=dst, send_sem=send_sem, recv_sem=recv_sem, device_id=device, device_id_type=MESH
        )
        copy.start()
        started.append(copy)

    def arrived(ref, sem):
        pltpu.make_async_copy(ref, ref, sem).wait()

    off = (0, -1, 1, 2)
    opp = (1, 0)

    def tile(arr, first, second, c):
        f, s = wrap((y, z)[arr] + first), wrap((z, y)[arr] + second)
        return rl.at[arr, f, s, c] if arr == 0 else rl.at[arr, s, f, c]

    def line(arr, second, c):
        s = wrap((z, y)[arr] + second)
        return rl.at[arr, :, s, c] if arr == 0 else rl.at[arr, s, :, c]

    def half(ref, d):
        rows = pl.ds(d * (SUB // 2), SUB // 2)
        return ref.at[rows] if len(ref.shape) == 2 else ref.at[:, rows]

    def s1_send(c):
        for d in (0, 1):
            for arr in (0, 1):
                ref = tile(arr, 0, 0, c)
                send(ref, ref, s1s.at[c, arr, d], s1r.at[c, arr, d], yz[arr][d])

    def s1_wait(c, d):
        for arr in (0, 1):
            arrived(tile(arr, -step[d], 0, c), s1r.at[c, arr, d])

    def s2_send(c, d):
        for arr in (0, 1):
            ref = half(tile(arr, -step[d], 0, c), d)
            send(ref, ref, s2s.at[c, arr, d], s2r.at[c, arr, d], yz[arr][d])

    def s2_wait(c):
        for arr in (0, 1):
            for d in (0, 1):
                arrived(half(tile(arr, 2, 0, c), d), s2r.at[c, arr, d])

    def s3_send(c, k):
        for d in (0, 1):
            for arr in (0, 1):
                ref = tile(arr, off[k], 0, c)
                send(ref, ref, s3s.at[c, arr, d, k], s3r.at[c, arr, d, k], yz[1 - arr][d])

    def s3_wait(c, k, d):
        for arr in (0, 1):
            arrived(tile(arr, off[k], -step[d], c), s3r.at[c, arr, d, k])

    def s4_send(c, k, d):
        for arr in (0, 1):
            ref = half(tile(arr, off[k], -step[d], c), d)
            send(ref, ref, s4s.at[c, arr, d, k], s4r.at[c, arr, d, k], yz[1 - arr][d])

    def s4_wait(c, k):
        for arr in (0, 1):
            for d in (0, 1):
                arrived(half(tile(arr, off[k], 2, c), d), s4r.at[c, arr, d, k])

    def s3_line_send(c):
        for d in (0, 1):
            for arr in (0, 1):
                ref = line(arr, 0, c)
                send(ref, ref, s3s.at[c, arr, d, 0], s3r.at[c, arr, d, 0], yz[1 - arr][d])

    def s4_line_send(c, lines):
        for d in (0, 1):
            for arr in (0, 1):
                if lines:
                    arrived(line(arr, -step[d], c), s3r.at[c, arr, d, 0])
                else:
                    for k in range(4):
                        arrived(tile(arr, off[k], -step[d], c), s3r.at[c, arr, d, k])
                ref = half(line(arr, -step[d], c), d)
                send(ref, ref, s4s.at[c, arr, d, 0], s4r.at[c, arr, d, 0], yz[1 - arr][d])

    def s4_line_wait(c):
        for arr in (0, 1):
            for d in (0, 1):
                arrived(half(line(arr, 2, c), d), s4r.at[c, arr, d, 0])

    def shard(dx, other=False):
        return wrap(x + dx) * 2 + (1 - core if other else core)

    def right_first():
        for d in (0, 1):
            for arr in (0, 1):
                send((rth, rtl)[arr], rr.at[arr, row], rs.at[0, arr, d], rv.at[0, arr, d], xs[d])
        for arr in (0, 1):
            send((rth, rtl)[arr], rr.at[arr, row], rs.at[1, arr, 0], rv.at[1, arr, 0], twin)

    def right_second(d):
        for arr in (0, 1):
            arrived(rr.at[arr, shard(-step[d])], rv.at[0, arr, d])
        ref = rr.at[d, shard(-step[d])]
        send(ref, ref, rs.at[2, d, 0], rv.at[2, d, 0], xs[d])
        for arr in (0, 1):
            ref = rr.at[arr, shard(-step[d])]
            send(ref, ref, rs.at[3 + d, arr, 0], rv.at[3 + d, arr, 0], twin)

    def right_third():
        for d in (0, 1):
            ref = rr.at[d, shard(2)]
            arrived(ref, rv.at[2, d, 0])
            send(ref, ref, rs.at[5, d, 0], rv.at[5, d, 0], twin)

    def split_right(index):
        rows = pl.multiple_of(index * RD, RD)
        for arr, base in ((0, 1024), (1, 0)):
            high, low = split(rr[arr, index])
            b[pl.ds(base + rows, RD), :] = high
            b[pl.ds(base + 512 + rows, RD), :] = low

    s1_send(0)
    right_first()
    s3_send(0, 0)
    for c in (1, 2, 3):
        s1_send(c)
    for copy in own_right:
        copy.wait()
    split_right(row)
    for d in (0, 1):
        s1_wait(0, d)
        s2_send(0, d)
    for k in (1, 2):
        s3_send(0, k)
    s2_wait(0)
    s3_send(0, 3)
    for c in (1, 2, 3):
        for d in (0, 1):
            s1_wait(c, d)
            s2_send(c, d)
    s3_send(1, 0)
    for arr in (0, 1):
        arrived(rr.at[arr, shard(0, True)], rv.at[1, arr, 0])
    split_right(shard(0, True))
    for d in (0, 1):
        right_second(d)
    for d in (0, 1):
        s3_wait(0, 0, d)
        s4_send(0, 0, d)
    for k in (1, 2):
        s3_send(1, k)
    for k in (1, 2):
        for d in (0, 1):
            s3_wait(0, k, d)
            s4_send(0, k, d)
    s2_wait(1)
    for d in (0, 1):
        s3_wait(0, 3, d)
        s4_send(0, 3, d)
    s3_send(1, 3)
    for d in (0, 1):
        split_right(shard(-step[d]))
    for d in (0, 1):
        for arr in (0, 1):
            arrived(rr.at[arr, shard(-step[d], True)], rv.at[3 + d, arr, 0])
        split_right(shard(-step[d], True))
    right_third()
    split_right(shard(2))
    for arr in (0, 1):
        arrived(rr.at[arr, shard(2, True)], rv.at[5, arr, 0])
    split_right(shard(2, True))
    s2_wait(2)
    s2_wait(3)

    lane = lax.broadcasted_iota(jnp.int32, (SUB, 128), 1) // KD

    def collect(c, target):
        def body(g, carry):
            for arr in (0, 1):
                for j in range(4):
                    value = rl[arr, g, (3 - j) % 4, c]
                    for p in range(3):
                        value = jnp.where(lane == p, rl[arr, g, (p - j) % 4, c], value)
                    if j:
                        value = pltpu.roll(value, 128 - KD * j, 1)
                    high, low = split(value)
                    cols = pl.multiple_of(arr * 1024 + g * 128, 128)
                    target[pl.ds(j * SUB, SUB), pl.ds(cols, 128)] = low
                    target[pl.ds(j * SUB, SUB), pl.ds(cols + 512, 128)] = high
            return carry

        lax.fori_loop(0, 4, body, 0)

    def multiply(c, u):
        src = pl.ds(u * 256, 256)
        dst = pl.ds(c * CH + u * 256, 256)
        out_h[dst, :] = times_hh(a, b, src)
        out_l[dst, :] = times_ll(a, b, src)
        out_c[dst, :] = times_cross(a, b, src)

    for c in range(EARLY):
        if c == 0:
            for k in range(4):
                s4_wait(0, k)
        else:
            s4_line_wait(c)
        if c + 2 < NCH:
            s3_line_send(c + 2)
        collect(c, a)
        multiply(c, 0)
        s4_line_send(c + 1, c + 1 >= 2)
        multiply(c, 1)
    s4_line_wait(EARLY)
    collect(EARLY, a_last)
    for copy in started:
        copy.wait_send()


def finish_kernel(c_in, h_in, l_in, a, b, c_out, h_out, l_out, stage, early_sem, late_sem):
    copies = []
    for i, (src, dst) in enumerate(((c_in, c_out), (h_in, h_out), (l_in, l_out))):
        for q in range(EARLY):
            rows = pl.ds(q * CH, CH)
            copies.append(pltpu.make_async_copy(src.at[rows], dst.at[rows], early_sem.at[i, q]))
            copies[-1].start()
    for u in range(2):
        rows = pl.ds(u * 256, 256)
        for i, (times, dst) in enumerate(((times_cross, c_out), (times_hh, h_out), (times_ll, l_out))):
            stage[i, rows] = times(a, b, rows)
            copies.append(
                pltpu.make_async_copy(
                    stage.at[i, rows], dst.at[pl.ds(EARLY * CH + u * 256, 256)], late_sem.at[i, u]
                )
            )
            copies[-1].start()
    for copy in copies:
        copy.wait()


def per_device(left_h, left_l, right_h, right_l):
    dma = pltpu.SemaphoreType.DMA
    hbm, vmem = pl.BlockSpec(memory_space=pl.ANY), pl.BlockSpec(memory_space=pltpu.VMEM)
    early = pl.pallas_call(
        gather_kernel,
        out_shape=[pltpu.VMEM((EARLY * CH, N), F32)] * 3
        + [pltpu.VMEM((CH, 4 * KW), BF16), pltpu.VMEM((4 * KW, N), BF16)],
        in_specs=[hbm] * 4,
        out_specs=[vmem] * 5,
        scratch_shapes=[
            pltpu.VMEM((2, KD, M), F32),
            pltpu.VMEM((2, 4, 4, NCH, SUB, 128), F32),
            pltpu.VMEM((2, 8, RD, N), F32),
            pltpu.VMEM((CH, 4 * KW), BF16),
            dma((4,)),
            dma((NCH, 2, 2)), dma((NCH, 2, 2)), dma((NCH, 2, 2)), dma((NCH, 2, 2)),
            dma((NCH, 2, 2, 4)), dma((NCH, 2, 2, 4)), dma((NCH, 2, 2, 4)), dma((NCH, 2, 2, 4)),
            dma((6, 2, 2)), dma((6, 2, 2)),
        ],
        compiler_params=pltpu.CompilerParams(
            collective_id=0, has_side_effects=True, vmem_limit_bytes=22 << 20
        ),
        cost_estimate=pl.CostEstimate(flops=18 * M * N * KW, bytes_accessed=2 << 20, transcendentals=0),
        name="gather_multiply",
    )(left_h.T, left_l.T, right_h, right_l)
    return pl.pallas_call(
        finish_kernel,
        out_shape=[jax.ShapeDtypeStruct((M, N), F32)] * 3,
        in_specs=[vmem] * 5,
        out_specs=[hbm] * 3,
        scratch_shapes=[pltpu.VMEM((3, CH, N), F32), dma((3, EARLY)), dma((3, 2))],
        compiler_params=pltpu.CompilerParams(vmem_limit_bytes=10 << 20),
        cost_estimate=pl.CostEstimate(flops=6 * M * N * KW, bytes_accessed=24 << 20, transcendentals=0),
        name="multiply_write",
    )(*(pltpu.with_memory_space_constraint(v, pltpu.VMEM) for v in early))


def solution(mesh):
    spec = P("row", "col")
    return jax.shard_map(
        per_device, mesh=mesh, in_specs=(spec,) * 4, out_specs=(spec,) * 3, check_vma=False
    )
```

time: 213 us -> 76.1 us (0.36)
  waiting for transfers between devices: 129 us -> 0 us
  Pallas kernels: 0 us -> 71.3 us
  matrix products: 69.3 us -> 0 us
  between operations: 13.8 us -> 0.83 us
  local copies, waits for them, and re-layouts: 0.01 us -> 3.79 us
    all_gather x4 -> x0, waiting for transfers between devices: 126 us -> none  [the longest x1 54.1 us: per_device(): lax.all_gather(left_l, 'col', axis=1, tiled=True)]
    pallas_call x0 -> x2, Pallas kernels: none -> 71.3 us  [the longest x1 62.8 us: per_device(): pl.pallas_call(gather_kernel, out_shape=[pltpu.VMEM((EARLY * CH, N), F32)...]
    dot_general x4 -> x0, matrix products: 69.3 us -> none  [product(): jnp.dot(left, right, preferred_element_type=jnp.float32, precision=lax.Pr...]
    unnamed x8, local copies, waits for them, and re-layouts: 0.01 us -> 3.79 us
    unnamed x4 -> x0, waiting for transfers between devices: 2.58 us -> none
  transfers between devices with their start and end apart: 4 -> 0, of which waited for: 4 -> 0; matrix products, arithmetic and copies ran while one was open for 17% -> 0% of each run, Pallas kernels for 0% -> 0%
where the time goes in v1:
time: 76.1 us; the launch traced here: 75.9 us
  Pallas kernels  71.3 us (94%)
  local copies, waits for them, and re-layouts  3.79 us (5%)
  between operations  0.83 us (1%)
    pallas_call x1, Pallas kernels, per_device(): pl.pallas_call(gather_kernel, out_shape=[pltpu.VMEM((EARLY * CH, N), F32)...  62.8 us
    pallas_call x1, Pallas kernels, per_device(): pl.pallas_call(finish_kernel, out_shape=[jax.ShapeDtypeStruct((M, N), F32...  8.48 us
    unnamed x8, local copies, waits for them, and re-layouts  3.79 us

profile of v1, /device:TPU:0, one launch (start us, length us, event | category | flops | bytes accessed | tf_op | source)
XLA Modules:
  0.0 75.9 jit_solution(16747225272791464535)
XLA Ops:
  0.6 0.0 copy-start
  0.6 0.9 %copy-done = f32[2048,32]{0,1:T(8,128)S(1)} copy-done((f32[2048,32]{0,1:T(8,128)S(1)}, f32[2048,32]{0,1:T(8,128)}, u32[]{:S(2)}) %copy-start) | copy-done | bytes 262168
  1.6 0.0 copy-start.1
  1.6 0.9 %copy-done.1 = f32[2048,32]{0,1:T(8,128)S(1)} copy-done((f32[2048,32]{0,1:T(8,128)S(1)}, f32[2048,32]{0,1:T(8,128)}, u32[]{:S(2)}) %copy-start.1) | copy-done | bytes 262168
  2.5 0.0 copy-start.2
  2.5 0.9 %copy-done.2 = f32[64,1024]{1,0:T(8,128)S(1)} copy-done((f32[64,1024]{1,0:T(8,128)S(1)}, f32[64,1024]{1,0:T(8,128)}, u32[]{:S(2)}) %copy-start.2) | copy-done | bytes 262168
  3.5 0.0 copy-start.3
  3.5 0.9 %copy-done.3 = f32[64,1024]{1,0:T(8,128)S(1)} copy-done((f32[64,1024]{1,0:T(8,128)S(1)}, f32[64,1024]{1,0:T(8,128)}, u32[]{:S(2)}) %copy-start.3) | copy-done | bytes 262168
  4.4 62.8 %gather_multiply.1 = (f32[1536,1024]{1,0:T(8,128)S(1)}, f32[1536,1024]{1,0:T(8,128)S(1)}, f32[1536,1024]{1,0:T(8,128)S(1)}, bf16[512,2048]{1,0:T(8,128)(2,1)S(1)}, bf16[2048,1024]{1,0:T(8,128)(2,1)S(1)}) custom-call(f32[32,2048]{1,0:T(8,128)S(1)} %bitcast.2, f32[32,2048]{1,0:T(8,128)S(1)} %bitcast.3, f32[64,1024]{1,0:T(8,128)S(1)} %copy-done.2, ...), custom_call_target="tpu_custom_call" | custom-call | flops 19327352832 | bytes 2097152 | tf_op jit(solution)/shard_map/gather_multiply/pallas_call | solution.py:324
  67.2 8.5 %multiply_write.1 = (f32[2048,1024]{1,0:T(8,128)}, f32[2048,1024]{1,0:T(8,128)}, f32[2048,1024]{1,0:T(8,128)}) custom-call(f32[1536,1024]{1,0:T(8,128)S(1)} %get-tuple-element.8.c_in, f32[1536,1024]{1,0:T(8,128)S(1)} %get-tuple-element.9.h_in, f32[1536,1024]{1,0:T(8,128)S(1)} %get-tuple-element.10.l_in, bf16[512,2048]{1,0:T(8,128)(2,1)S(1)} %get-tuple-element.11.a, ...), custom_call_target="tpu_custom_call" | custom-call | flops 6442450944 | bytes 25165824 | tf_op jit(solution)/shard_map/multiply_write/pallas_call | solution.py:346
Async XLA Ops:
  0.6 1.0 %copy-start = (f32[2048,32]{0,1:T(8,128)S(1)}, f32[2048,32]{0,1:T(8,128)}, u32[]{:S(2)}) copy-start(f32[2048,32]{0,1:T(8,128)} %param.4) | copy-start | bytes 786436
  1.6 0.9 %copy-start.1 = (f32[2048,32]{0,1:T(8,128)S(1)}, f32[2048,32]{0,1:T(8,128)}, u32[]{:S(2)}) copy-start(f32[2048,32]{0,1:T(8,128)} %param.5) | copy-start | bytes 786436
  2.5 0.9 %copy-start.2 = (f32[64,1024]{1,0:T(8,128)S(1)}, f32[64,1024]{1,0:T(8,128)}, u32[]{:S(2)}) copy-start(f32[64,1024]{1,0:T(8,128)} %rth.1) | copy-start | bytes 786436
  3.5 0.9 %copy-start.3 = (f32[64,1024]{1,0:T(8,128)S(1)}, f32[64,1024]{1,0:T(8,128)}, u32[]{:S(2)}) copy-start(f32[64,1024]{1,0:T(8,128)} %rtl.1) | copy-start | bytes 786436

commit v2 on v1

v2 whole, which is shorter than its diff:
```python
import functools

import jax
import jax.numpy as jnp
from jax import lax
from jax.experimental import pallas as pl
from jax.experimental.pallas import tpu as pltpu
from jax.sharding import PartitionSpec as P

KW = 512
SCALE = 2.0**30 / KW
MESH = pl.DeviceIdType.MESH
F32, BF16 = jnp.float32, jnp.bfloat16

M, N, KD, RD = 2048, 1024, 32, 64
CH = 512
NCH = M // CH
EARLY = NCH - 1
SUB = CH // 4

dot = functools.partial(jnp.dot, preferred_element_type=F32)


def split(value):
    high = value.astype(BF16)
    return high, (value - high.astype(F32)).astype(BF16)


def times_hh(a, b, rows):
    return SCALE * (dot(a[rows, 0:1024], b[1024:2048, :]) + dot(a[rows, 512:1024], b[1024:1536, :]))


def times_ll(a, b, rows):
    return SCALE * (dot(a[rows, 1024:2048], b[0:1024, :]) + dot(a[rows, 1536:2048], b[0:512, :]))


def times_cross(a, b, rows):
    small = dot(a[rows, :], b[:, :])
    return SCALE * (small + (dot(a[rows, 512:1024], b[0:512, :]) + dot(a[rows, 1536:2048], b[1024:1536, :])))


def gather_kernel(
    lth, ltl, rth, rtl,
    out_c, out_h, out_l, a_last, b,
    lt, rl, rr, a, load_sem,
    near_sent, far_sent, right_sent, s1r, s2r, s3r, s4r, rv,
):
    row, col = lax.axis_index("row"), lax.axis_index("col")
    x, core, y, z = row // 2, row % 2, col // 4, col % 4

    def wrap(v):
        return lax.rem(v + 8, 4)

    def at(dx=0, dc=0, dy=0, dz=0):
        new_core = 1 - core if dc else core
        return (wrap(x + dx) * 2 + new_core, wrap(y + dy) * 4 + wrap(z + dz))

    step = (1, -1)
    yz = tuple(tuple(at(dy=d) if ax == 0 else at(dz=d) for d in step) for ax in (0, 1))
    xs = tuple(at(dx=d) for d in step)
    twin = at(dc=1)

    loads = [pltpu.make_async_copy(ref, lt.at[i], load_sem.at[i]) for i, ref in enumerate((lth, ltl))]
    own_right = [pltpu.make_async_copy(ref, rr.at[i, row], load_sem.at[2 + i]) for i, ref in enumerate((rth, rtl))]
    for copy in loads + own_right:
        copy.start()
    barrier = pltpu.get_barrier_semaphore()
    for device in (*yz[0], *yz[1], *xs, twin):
        pl.semaphore_signal(barrier, 1, device_id=device, device_id_type=MESH)
    for copy in loads:
        copy.wait()

    def pack(c):
        for arr in (0, 1):
            parts = []
            for p in range(4):
                start = pl.multiple_of(c * CH + wrap(p - z) * SUB, SUB)
                parts.append(lt[arr, :, pl.ds(start, SUB)])
            rl[arr, y, z, c] = jnp.concatenate(parts, axis=0).T

    pack(0)
    pl.semaphore_wait(barrier, 7)

    def send(src, dst, send_sem, recv_sem, device):
        pltpu.make_async_remote_copy(
            src_ref=src, dst_ref=dst, send_sem=send_sem, recv_sem=recv_sem, device_id=device, device_id_type=MESH
        ).start()

    def arrived(ref, sem):
        pltpu.make_async_copy(ref, ref, sem).wait()

    off = (0, -1, 1, 2)
    both = [(d, arr) for d in (0, 1) for arr in (0, 1)]

    def tile(arr, first, second, c):
        f, s = wrap((y, z)[arr] + first), wrap((z, y)[arr] + second)
        return rl.at[arr, f, s, c] if arr == 0 else rl.at[arr, s, f, c]

    def line(arr, second, c):
        s = wrap((z, y)[arr] + second)
        return rl.at[arr, :, s, c] if arr == 0 else rl.at[arr, s, :, c]

    def half(ref, d):
        rows = pl.ds(d * (SUB // 2), SUB // 2)
        return ref.at[rows] if len(ref.shape) == 2 else ref.at[:, rows]

    def s1_send(c):
        for d, arr in both:
            ref = tile(arr, 0, 0, c)
            send(ref, ref, near_sent.at[0], s1r.at[c], yz[arr][d])

    def s2_send(c):
        arrived(rl.at[0, 0, :, c], s1r.at[c])
        for d, arr in both:
            ref = half(tile(arr, -step[d], 0, c), d)
            send(ref, ref, near_sent.at[0], s2r.at[c], yz[arr][d])

    def s2_wait(c):
        arrived(rl.at[0, 0, 0:2, c], s2r.at[c])

    def s3_send(c, k, sem):
        for d, arr in both:
            ref = tile(arr, off[k], 0, c)
            send(ref, ref, far_sent.at[0], s3r.at[sem], yz[1 - arr][d])

    def s4_send(c, k, sem):
        arrived(rl.at[0, 0, :, c], s3r.at[sem])
        for d, arr in both:
            ref = half(tile(arr, off[k], -step[d], c), d)
            send(ref, ref, far_sent.at[0], s4r.at[c], yz[1 - arr][d])

    def s3_line_send(c, sem):
        for d, arr in both:
            ref = line(arr, 0, c)
            send(ref, ref, far_sent.at[0], s3r.at[sem], yz[1 - arr][d])

    def s4_line_send(c, sem):
        arrived(rl.at[0, :, :, c], s3r.at[sem])
        for d, arr in both:
            ref = half(line(arr, -step[d], c), d)
            send(ref, ref, far_sent.at[0], s4r.at[c], yz[1 - arr][d])

    def s4_wait(c):
        arrived(rl.at[0, 0:2, :, c], s4r.at[c])

    def shard(dx, other=False):
        return wrap(x + dx) * 2 + (1 - core if other else core)

    def right_first():
        for arr, d in ((0, 0), (1, 1), (1, 0), (0, 1)):
            send((rth, rtl)[arr], rr.at[arr, row], right_sent.at[0], rv.at[arr * 2 + d], xs[d])
        for arr in (0, 1):
            send((rth, rtl)[arr], rr.at[arr, row], right_sent.at[0], rv.at[4], twin)

    def right_across(arr, dx, sem):
        ref = rr.at[arr, shard(dx)]
        send(ref, ref, right_sent.at[0], rv.at[sem], twin)

    def right_second(d):
        ref = rr.at[d, shard(-step[d])]
        arrived(ref, rv.at[d * 3])
        send(ref, ref, right_sent.at[0], rv.at[5 + d], xs[d])
        right_across(d, -step[d], 7 + d)

    def right_second_rest(d):
        arr = 1 - d
        arrived(rr.at[arr, shard(-step[d])], rv.at[arr * 2 + d])
        right_across(arr, -step[d], 7 + d)

    def right_third(d):
        arrived(rr.at[d, shard(2)], rv.at[5 + d])
        right_across(d, 2, 9)

    def right_crossed(dx, sem):
        arrived(rr.at[:, shard(dx, True)], rv.at[sem])
        split_right(shard(dx, True))

    def split_right(index):
        rows = pl.multiple_of(index * RD, RD)
        for arr, base in ((0, 1024), (1, 0)):
            high, low = split(rr[arr, index])
            b[pl.ds(base + rows, RD), :] = high
            b[pl.ds(base + 512 + rows, RD), :] = low

    s1_send(0)
    right_first()
    s3_send(0, 0, 0)
    for c in (1, 2, 3):
        pack(c)
        s1_send(c)
    for copy in own_right:
        copy.wait()
    split_right(row)
    s2_send(0)
    for k in (1, 2):
        s3_send(0, k, k)
    right_crossed(0, 4)
    s2_send(1)
    s2_wait(0)
    s3_send(0, 3, 3)
    for c in (2, 3):
        s2_send(c)
    s3_send(1, 0, 4)
    s4_send(0, 0, 0)
    for d in (0, 1):
        right_second(d)
    for k in (1, 2):
        s3_send(1, k, 4)
        s4_send(0, k, k)
    s2_wait(1)
    s3_send(1, 3, 4)
    for d in (0, 1):
        right_second_rest(d)
    s4_send(0, 3, 3)
    s2_wait(2)
    s3_line_send(2, 5)
    for d in (0, 1):
        split_right(shard(-step[d]))
    for d in (0, 1):
        right_crossed(-step[d], 7 + d)
    for d in (0, 1):
        right_third(d)
    split_right(shard(2))
    right_crossed(2, 9)
    s2_wait(3)

    lane = lax.broadcasted_iota(jnp.int32, (SUB, 128), 1) // KD

    def collect(c, target):
        def body(g, carry):
            for arr in (0, 1):
                for j in range(4):
                    value = rl[arr, g, (3 - j) % 4, c]
                    for p in range(3):
                        value = jnp.where(lane == p, rl[arr, g, (p - j) % 4, c], value)
                    if j:
                        value = pltpu.roll(value, 128 - KD * j, 1)
                    high, low = split(value)
                    cols = pl.multiple_of(arr * 1024 + g * 128, 128)
                    target[pl.ds(j * SUB, SUB), pl.ds(cols, 128)] = low
                    target[pl.ds(j * SUB, SUB), pl.ds(cols + 512, 128)] = high
            return carry

        lax.fori_loop(0, 4, body, 0)

    def multiply(c, u):
        src = pl.ds(u * 256, 256)
        dst = pl.ds(c * CH + u * 256, 256)
        out_h[dst, :] = times_hh(a, b, src)
        yield
        out_l[dst, :] = times_ll(a, b, src)
        yield
        out_c[dst, :] = times_cross(a, b, src)
        yield

    def chunk(c, events):
        collect(c, a)
        n = 0
        for u in (0, 1):
            for _ in multiply(c, u):
                if n in events:
                    events[n]()
                n += 1

    s4_wait(0)

    def second():
        s4_line_send(1, 4)
        s3_send(3, 0, 6)

    chunk(0, {2: second})
    s4_wait(1)

    def third():
        s4_line_send(2, 5)
        for k in (1, 2, 3):
            s3_send(3, k, 6 + k)

    chunk(1, {1: third})
    s4_wait(2)
    chunk(2, {k: functools.partial(s4_send, 3, k, 6 + k) for k in range(4)})
    s4_wait(3)
    collect(EARLY, a_last)
    arrived(rl.at[:, :, 0:3, 0], near_sent.at[0])
    arrived(rl.at[:, :, :, 0:3], far_sent.at[0])
    arrived(rr.at[:, 0:7], right_sent.at[0])


def finish_kernel(c_in, h_in, l_in, a, b, c_out, h_out, l_out, stage, early_sem, late_sem):
    copies = []
    for i, (src, dst) in enumerate(((c_in, c_out), (h_in, h_out), (l_in, l_out))):
        for q in range(EARLY):
            rows = pl.ds(q * CH, CH)
            copies.append(pltpu.make_async_copy(src.at[rows], dst.at[rows], early_sem.at[i, q]))
            copies[-1].start()
    for u in range(2):
        rows = pl.ds(u * 256, 256)
        for i, (times, dst) in enumerate(((times_cross, c_out), (times_hh, h_out), (times_ll, l_out))):
            stage[i, rows] = times(a, b, rows)
            copies.append(
                pltpu.make_async_copy(
                    stage.at[i, rows], dst.at[pl.ds(EARLY * CH + u * 256, 256)], late_sem.at[i, u]
                )
            )
            copies[-1].start()
    for copy in copies:
        copy.wait()


def per_device(left_h, left_l, right_h, right_l):
    dma = pltpu.SemaphoreType.DMA
    hbm, vmem = pl.BlockSpec(memory_space=pl.ANY), pl.BlockSpec(memory_space=pltpu.VMEM)
    early = pl.pallas_call(
        gather_kernel,
        out_shape=[pltpu.VMEM((EARLY * CH, N), F32)] * 3
        + [pltpu.VMEM((CH, 4 * KW), BF16), pltpu.VMEM((4 * KW, N), BF16)],
        in_specs=[hbm] * 4,
        out_specs=[vmem] * 5,
        scratch_shapes=[
            pltpu.VMEM((2, KD, M), F32),
            pltpu.VMEM((2, 4, 4, NCH, SUB, 128), F32),
            pltpu.VMEM((2, 8, RD, N), F32),
            pltpu.VMEM((CH, 4 * KW), BF16),
            dma((4,)),
            dma((1,)), dma((1,)), dma((1,)), dma((NCH,)), dma((NCH,)), dma((10,)), dma((NCH,)), dma((10,)),
        ],
        compiler_params=pltpu.CompilerParams(
            collective_id=0, has_side_effects=True, vmem_limit_bytes=22 << 20
        ),
        cost_estimate=pl.CostEstimate(flops=18 * M * N * KW, bytes_accessed=2 << 20, transcendentals=0),
        name="gather_multiply",
    )(*(pltpu.with_memory_space_constraint(v, pltpu.HBM) for v in (left_h.T, left_l.T, right_h, right_l)))
    return pl.pallas_call(
        finish_kernel,
        out_shape=[jax.ShapeDtypeStruct((M, N), F32)] * 3,
        in_specs=[vmem] * 5,
        out_specs=[hbm] * 3,
        scratch_shapes=[pltpu.VMEM((3, CH, N), F32), dma((3, EARLY)), dma((3, 2))],
        compiler_params=pltpu.CompilerParams(vmem_limit_bytes=10 << 20),
        cost_estimate=pl.CostEstimate(flops=6 * M * N * KW, bytes_accessed=24 << 20, transcendentals=0),
        name="multiply_write",
    )(*(pltpu.with_memory_space_constraint(v, pltpu.VMEM) for v in early))


def solution(mesh):
    spec = P("row", "col")
    return jax.shard_map(
        per_device, mesh=mesh, in_specs=(spec,) * 4, out_specs=(spec,) * 3, check_vma=False
    )
```

time: 76.1 us -> 68.6 us (0.901)
  local copies, waits for them, and re-layouts: 3.79 us -> 0 us
  Pallas kernels: 71.3 us -> 67.7 us
    unnamed x8 -> x0, local copies, waits for them, and re-layouts: 3.79 us -> none
    pallas_call x1, Pallas kernels: 62.8 us -> 59.2 us  [per_device(): pl.pallas_call(gather_kernel, out_shape=[pltpu.VMEM((EARLY * CH, N), F32)...]
where the time goes in v2:
time: 68.6 us; the launch traced here: 68.5 us
  Pallas kernels  67.7 us (99%)
  between operations  0.8 us (1%)
    pallas_call x1, Pallas kernels, per_device(): pl.pallas_call(gather_kernel, out_shape=[pltpu.VMEM((EARLY * CH, N), F32)...  59.2 us
    pallas_call x1, Pallas kernels, per_device(): pl.pallas_call(finish_kernel, out_shape=[jax.ShapeDtypeStruct((M, N), F32...  8.48 us

profile of v2, /device:TPU:0, one launch (start us, length us, event | category | flops | bytes accessed | tf_op | source)
XLA Modules:
  0.0 68.5 jit_solution(4842320826446869517)
XLA Ops:
  0.6 59.2 %gather_multiply.1 = (f32[1536,1024]{1,0:T(8,128)S(1)}, f32[1536,1024]{1,0:T(8,128)S(1)}, f32[1536,1024]{1,0:T(8,128)S(1)}, bf16[512,2048]{1,0:T(8,128)(2,1)S(1)}, bf16[2048,1024]{1,0:T(8,128)(2,1)S(1)}) custom-call(f32[32,2048]{1,0:T(8,128)} %bitcast.2, f32[32,2048]{1,0:T(8,128)} %bitcast.3, f32[64,1024]{1,0:T(8,128)} %rth.1, f32[64,1024]{1,0:T(8,128)} %rtl.1), custom_call_target="tpu_custom_call" | custom-call | flops 19327352832 | bytes 2097152 | tf_op jit(solution)/shard_map/gather_multiply/pallas_call | solution.py:313
  59.8 8.5 %multiply_write.1 = (f32[2048,1024]{1,0:T(8,128)}, f32[2048,1024]{1,0:T(8,128)}, f32[2048,1024]{1,0:T(8,128)}) custom-call(f32[1536,1024]{1,0:T(8,128)S(1)} %get-tuple-element.8.c_in, f32[1536,1024]{1,0:T(8,128)S(1)} %get-tuple-element.9.h_in, f32[1536,1024]{1,0:T(8,128)S(1)} %get-tuple-element.10.l_in, bf16[512,2048]{1,0:T(8,128)(2,1)S(1)} %get-tuple-element.11.a, ...), custom_call_target="tpu_custom_call" | custom-call | flops 6442450944 | bytes 25165824 | tf_op jit(solution)/shard_map/multiply_write/pallas_call | solution.py:333

commit v3 on v2

v3 whole, which is shorter than its diff:
```python
import functools

import jax
import jax.numpy as jnp
from jax import lax
from jax.experimental import pallas as pl
from jax.experimental.pallas import tpu as pltpu
from jax.sharding import PartitionSpec as P

KW = 512
SCALE = 2.0**30 / KW
MESH = pl.DeviceIdType.MESH
F32, BF16 = jnp.float32, jnp.bfloat16

M, N, KD, RD = 2048, 1024, 32, 64
CH = 512
NCH = M // CH
SUB = CH // 4
BLK = 32
LATE = CH
EARLY = M - LATE

dot = functools.partial(jnp.dot, preferred_element_type=F32)


def split(value):
    high = value.astype(BF16)
    return high, (value - high.astype(F32)).astype(BF16)


def times_hh(a, b, rows):
    return SCALE * (dot(a[rows, 0:1024], b[1024:2048, :]) + dot(a[rows, 512:1024], b[1024:1536, :]))


def times_ll(a, b, rows):
    return SCALE * (dot(a[rows, 1024:2048], b[0:1024, :]) + dot(a[rows, 1536:2048], b[0:512, :]))


def times_cross(a, b, rows):
    small = dot(a[rows, :], b[:, :])
    return SCALE * (small + (dot(a[rows, 512:1024], b[0:512, :]) + dot(a[rows, 1536:2048], b[1024:1536, :])))


def collect(tiles, target):
    lane = lax.broadcasted_iota(jnp.int32, (BLK, 128), 1) // KD

    def body(g, carry):
        for arr in (0, 1):
            cols = pl.multiple_of(arr * 1024 + g * 128, 128)
            for r in range(0, SUB, BLK):
                source = [tiles[arr, g, q, pl.ds(r, BLK)] for q in range(4)]
                for j in range(4):
                    value = source[(3 - j) % 4]
                    for p in range(3):
                        value = jnp.where(lane == p, source[(p - j) % 4], value)
                    if j:
                        value = pltpu.roll(value, 128 - KD * j, 1)
                    high, low = split(value)
                    rows = pl.ds(j * SUB + r, BLK)
                    target[rows, pl.ds(cols, 128)] = low
                    target[rows, pl.ds(cols + 512, 128)] = high
        return carry

    lax.fori_loop(0, 4, body, 0)


def gather_kernel(
    lth, ltl, rth, rtl,
    out_c, out_h, out_l, rl_last, b,
    lt, rl, rr, a, load_sem,
    near_sent, far_sent, right_sent, s1r, s2r, s3r, s4r, rv,
):
    row, col = lax.axis_index("row"), lax.axis_index("col")
    x, core, y, z = row // 2, row % 2, col // 4, col % 4

    def wrap(v):
        return lax.rem(v + 8, 4)

    def at(dx=0, dc=0, dy=0, dz=0):
        new_core = 1 - core if dc else core
        return (wrap(x + dx) * 2 + new_core, wrap(y + dy) * 4 + wrap(z + dz))

    step = (1, -1)
    yz = tuple(tuple(at(dy=d) if ax == 0 else at(dz=d) for d in step) for ax in (0, 1))
    xs = tuple(at(dx=d) for d in step)
    twin = at(dc=1)

    loads = [pltpu.make_async_copy(ref, lt.at[i], load_sem.at[i]) for i, ref in enumerate((lth, ltl))]
    own_right = [pltpu.make_async_copy(ref, rr.at[i, row], load_sem.at[2 + i]) for i, ref in enumerate((rth, rtl))]
    for copy in loads + own_right:
        copy.start()
    barrier = pltpu.get_barrier_semaphore()
    for device in (*yz[0], *yz[1], *xs, twin):
        pl.semaphore_signal(barrier, 1, device_id=device, device_id_type=MESH)
    for copy in loads:
        copy.wait()

    def chunk(c):
        return rl_last if c == NCH - 1 else rl.at[c]

    def pack(c):
        for arr in (0, 1):
            parts = []
            for p in range(4):
                start = pl.multiple_of(c * CH + wrap(p - z) * SUB, SUB)
                parts.append(lt[arr, :, pl.ds(start, SUB)])
            chunk(c)[arr, y, z] = jnp.concatenate(parts, axis=0).T

    pack(0)
    pl.semaphore_wait(barrier, 7)

    def send(src, dst, send_sem, recv_sem, device):
        pltpu.make_async_remote_copy(
            src_ref=src, dst_ref=dst, send_sem=send_sem, recv_sem=recv_sem, device_id=device, device_id_type=MESH
        ).start()

    def arrived(ref, sem):
        pltpu.make_async_copy(ref, ref, sem).wait()

    off = (0, -1, 1, 2)
    both = [(d, arr) for d in (0, 1) for arr in (0, 1)]

    def tile(arr, first, second, c):
        f, s = wrap((y, z)[arr] + first), wrap((z, y)[arr] + second)
        return chunk(c).at[arr, f, s] if arr == 0 else chunk(c).at[arr, s, f]

    def half(ref, d):
        return ref.at[pl.ds(d * (SUB // 2), SUB // 2)]

    def s1_send(c):
        for d, arr in both:
            ref = tile(arr, 0, 0, c)
            send(ref, ref, near_sent.at[0], s1r.at[c], yz[arr][d])

    def s2_send(c):
        arrived(rl.at[0, 0, 0], s1r.at[c])
        for d, arr in both:
            ref = half(tile(arr, -step[d], 0, c), d)
            send(ref, ref, near_sent.at[0], s2r.at[c], yz[arr][d])

    def s2_wait(c):
        arrived(rl.at[0, 0, 0, 0:2], s2r.at[c])

    def s3_send(c, *ks):
        for k in ks:
            for d, arr in both:
                ref = tile(arr, off[k], 0, c)
                send(ref, ref, far_sent.at[0], s3r.at[c, k], yz[1 - arr][d])

    def s4_send(c, *ks):
        for k in ks:
            arrived(rl.at[0, 0, 0], s3r.at[c, k])
            for d, arr in both:
                ref = half(tile(arr, off[k], -step[d], c), d)
                send(ref, ref, far_sent.at[0], s4r.at[c], yz[1 - arr][d])

    def s4_wait(c):
        arrived(rl.at[0, 0, 0:2], s4r.at[c])

    def shard(dx, other=False):
        return wrap(x + dx) * 2 + (1 - core if other else core)

    def right_first():
        for arr, d in ((0, 0), (1, 1), (1, 0), (0, 1)):
            send((rth, rtl)[arr], rr.at[arr, row], right_sent.at[0], rv.at[arr * 2 + d], xs[d])
        for arr in (0, 1):
            send((rth, rtl)[arr], rr.at[arr, row], right_sent.at[0], rv.at[4], twin)

    def right_across(arr, dx, sem):
        ref = rr.at[arr, shard(dx)]
        send(ref, ref, right_sent.at[0], rv.at[sem], twin)

    def right_second(d):
        ref = rr.at[d, shard(-step[d])]
        arrived(ref, rv.at[d * 3])
        send(ref, ref, right_sent.at[0], rv.at[5 + d], xs[d])
        right_across(d, -step[d], 7 + d)

    def right_second_rest(d):
        arr = 1 - d
        arrived(rr.at[arr, shard(-step[d])], rv.at[arr * 2 + d])
        right_across(arr, -step[d], 7 + d)

    def right_third(d):
        arrived(rr.at[d, shard(2)], rv.at[5 + d])
        right_across(d, 2, 9)

    def right_crossed(dx, sem):
        arrived(rr.at[:, shard(dx, True)], rv.at[sem])
        split_right(shard(dx, True))

    def split_right(index):
        rows = pl.multiple_of(index * RD, RD)
        for arr, base in ((0, 1024), (1, 0)):
            high, low = split(rr[arr, index])
            b[pl.ds(base + rows, RD), :] = high
            b[pl.ds(base + 512 + rows, RD), :] = low

    s1_send(0)
    right_first()
    s3_send(0, 0)
    pack(1)
    s1_send(1)
    pack(2)
    pack(3)
    for copy in own_right:
        copy.wait()
    split_right(row)
    s2_send(0)
    s3_send(0, 1, 2)
    s1_send(2)
    right_crossed(0, 4)
    s2_wait(0)
    s3_send(0, 3)
    s2_send(1)
    s4_send(0, 0)
    for d in (0, 1):
        right_second(d)
    s4_send(0, 1, 2)
    s3_send(1, 0)
    s2_send(2)
    s4_send(0, 3)
    s3_send(1, 1, 2)
    s2_wait(1)
    s3_send(1, 3)
    s1_send(3)
    s3_send(2, 0)
    for d in (0, 1):
        right_second_rest(d)
    for d in (0, 1):
        split_right(shard(-step[d]))
    for d in (0, 1):
        right_crossed(-step[d], 7 + d)
    s4_send(1, 0)
    s4_wait(0)
    collect(rl.at[0], a)
    for d in (0, 1):
        right_third(d)
    split_right(shard(2))
    right_crossed(2, 9)
    s2_wait(2)

    def multiply(start, events):
        n = 0
        for u in range(0, CH, 256):
            src, dst = pl.ds(u, 256), pl.ds(start + u, 256)
            for out, times in ((out_h, times_hh), (out_l, times_ll), (out_c, times_cross)):
                out[dst, :] = times(a, b, src)
                for step_, *given in events.get(n, ()):
                    step_(*given)
                n += 1

    multiply(
        0,
        {
            1: ((s4_send, 1, 1, 2),),
            2: ((s4_send, 1, 3), (s3_send, 2, 1, 2, 3)),
            3: ((s2_send, 3), (s3_send, 3, 0)),
        },
    )
    s4_wait(1)
    collect(rl.at[1], a)
    multiply(
        CH,
        {
            1: ((s4_send, 2, 0, 1),),
            2: ((s4_send, 2, 2, 3), (s3_send, 3, 1, 2)),
            3: ((s2_wait, 3), (s3_send, 3, 3)),
            5: ((s4_send, 3, 0),),
        },
    )
    s4_wait(2)
    collect(rl.at[2], a)
    multiply(2 * CH, {0: ((s4_send, 3, 1),), 1: ((s4_send, 3, 2),), 2: ((s4_send, 3, 3),)})
    s4_wait(3)
    arrived(rl.at[0, :, :, 0:3], near_sent.at[0])
    arrived(rl, far_sent.at[0])
    arrived(rr.at[:, 0:7], right_sent.at[0])


def finish_kernel(c_in, h_in, l_in, tiles, b, c_out, h_out, l_out, a, stage, early_sem, late_sem):
    copies = []
    for i, (src, dst) in enumerate(((c_in, c_out), (h_in, h_out), (l_in, l_out))):
        for q, start in enumerate(range(0, EARLY, CH)):
            rows = pl.ds(start, min(CH, EARLY - start))
            copies.append(pltpu.make_async_copy(src.at[rows], dst.at[rows], early_sem.at[i, q]))
            copies[-1].start()
    collect(tiles, a)
    for u in range(2):
        rows = pl.ds(u * (LATE // 2), LATE // 2)
        for i, (times, dst) in enumerate(((times_cross, c_out), (times_hh, h_out), (times_ll, l_out))):
            stage[i, rows] = times(a, b, rows)
            copies.append(
                pltpu.make_async_copy(
                    stage.at[i, rows], dst.at[pl.ds(EARLY + u * (LATE // 2), LATE // 2)], late_sem.at[i, u]
                )
            )
            copies[-1].start()
    for copy in copies:
        copy.wait()


def per_device(left_h, left_l, right_h, right_l):
    dma = pltpu.SemaphoreType.DMA
    hbm, vmem = pl.BlockSpec(memory_space=pl.ANY), pl.BlockSpec(memory_space=pltpu.VMEM)
    early = pl.pallas_call(
        gather_kernel,
        out_shape=[pltpu.VMEM((EARLY, N), F32)] * 3
        + [pltpu.VMEM((2, 4, 4, SUB, 128), F32), pltpu.VMEM((4 * KW, N), BF16)],
        in_specs=[hbm] * 4,
        out_specs=[vmem] * 5,
        scratch_shapes=[
            pltpu.VMEM((2, KD, M), F32),
            pltpu.VMEM((NCH - 1, 2, 4, 4, SUB, 128), F32),
            pltpu.VMEM((2, 8, RD, N), F32),
            pltpu.VMEM((CH, 4 * KW), BF16),
            dma((4,)),
            dma((1,)), dma((1,)), dma((1,)), dma((NCH,)), dma((NCH,)), dma((NCH, 4)), dma((NCH,)), dma((10,)),
        ],
        compiler_params=pltpu.CompilerParams(
            collective_id=0, has_side_effects=True, vmem_limit_bytes=22 << 20
        ),
        cost_estimate=pl.CostEstimate(flops=24 * EARLY * N * KW, bytes_accessed=2 << 20, transcendentals=0),
        name="gather_multiply",
    )(*(pltpu.with_memory_space_constraint(v, pltpu.HBM) for v in (left_h.T, left_l.T, right_h, right_l)))
    return pl.pallas_call(
        finish_kernel,
        out_shape=[jax.ShapeDtypeStruct((M, N), F32)] * 3,
        in_specs=[vmem] * 5,
        out_specs=[hbm] * 3,
        scratch_shapes=[pltpu.VMEM((LATE, 4 * KW), BF16), pltpu.VMEM((3, LATE, N), F32), dma((3, 3)), dma((3, 2))],
        compiler_params=pltpu.CompilerParams(vmem_limit_bytes=12 << 20),
        cost_estimate=pl.CostEstimate(flops=24 * LATE * N * KW, bytes_accessed=24 << 20, transcendentals=0),
        name="multiply_write",
    )(*(pltpu.with_memory_space_constraint(v, pltpu.VMEM) for v in early))


def solution(mesh):
    spec = P("row", "col")
    return jax.shard_map(
        per_device, mesh=mesh, in_specs=(spec,) * 4, out_specs=(spec,) * 3, check_vma=False
    )
```

time: 68.6 us -> 63.5 us (0.926)
  the two profiles are of different devices: /device:TPU:0 before, /device:TPU:1 now
where the time goes in v3:
time: 63.5 us; the launch traced here: 63.4 us
  Pallas kernels  62.6 us (99%)
  between operations  0.8 us (1%)
    pallas_call x1, Pallas kernels, per_device(): pl.pallas_call(gather_kernel, out_shape=[pltpu.VMEM((EARLY, N), F32)] * 3...  54.1 us
    pallas_call x1, Pallas kernels, per_device(): pl.pallas_call(finish_kernel, out_shape=[jax.ShapeDtypeStruct((M, N), F32...  8.51 us

profile of v3, /device:TPU:1, one launch (start us, length us, event | category | flops | bytes accessed | tf_op | source)
XLA Modules:
  0.0 63.4 jit_solution(14372088762469028027)
XLA Ops:
  0.6 54.1 %gather_multiply.1 = (f32[1536,1024]{1,0:T(8,128)S(1)}, f32[1536,1024]{1,0:T(8,128)S(1)}, f32[1536,1024]{1,0:T(8,128)S(1)}, f32[2,4,4,128,128]{4,3,2,1,0:T(8,128)S(1)}, bf16[2048,1024]{1,0:T(8,128)(2,1)S(1)}) custom-call(f32[32,2048]{1,0:T(8,128)} %bitcast.2, f32[32,2048]{1,0:T(8,128)} %bitcast.3, f32[64,1024]{1,0:T(8,128)} %rth.1, f32[64,1024]{1,0:T(8,128)} %rtl.1), custom_call_target="tpu_custom_call" | custom-call | flops 19327352832 | bytes 2097152 | tf_op jit(solution)/shard_map/gather_multiply/pallas_call | solution.py:306
  54.7 8.5 %multiply_write.1 = (f32[2048,1024]{1,0:T(8,128)}, f32[2048,1024]{1,0:T(8,128)}, f32[2048,1024]{1,0:T(8,128)}) custom-call(f32[1536,1024]{1,0:T(8,128)S(1)} %get-tuple-element.8.c_in, f32[1536,1024]{1,0:T(8,128)S(1)} %get-tuple-element.9.h_in, f32[1536,1024]{1,0:T(8,128)S(1)} %get-tuple-element.10.l_in, f32[2,4,4,128,128]{4,3,2,1,0:T(8,128)S(1)} %get-tuple-element.11.tiles, ...), custom_call_target="tpu_custom_call" | custom-call | flops 6442450944 | bytes 25165824 | tf_op jit(solution)/shard_map/multiply_write/pallas_call | solution.py:326

commit v4 on v3

--- a/solution.py
+++ b/solution.py
@@ -39,6 +39,12 @@
 def times_cross(a, b, rows):
     small = dot(a[rows, :], b[:, :])
     return SCALE * (small + (dot(a[rows, 512:1024], b[0:512, :]) + dot(a[rows, 1536:2048], b[1024:1536, :])))
+
+
+def times_part(a, b, rows, start, left, right):
+    low, high = a[rows, pl.ds(left + start, 256)], a[rows, pl.ds(left + 512 + start, 256)]
+    b_high, b_low = b[pl.ds(right + start, 256), :], b[pl.ds(right + 512 + start, 256), :]
+    return dot(low, b_high) + dot(high, b_low) + dot(high, b_high)
 
 
 def collect(tiles, target):
@@ -234,27 +240,51 @@
     s4_send(1, 0)
     s4_wait(0)
     collect(rl.at[0], a)
-    for d in (0, 1):
-        right_third(d)
-    split_right(shard(2))
-    right_crossed(2, 9)
-    s2_wait(2)
-
-    def multiply(start, events):
+
+    def after(events, n):
+        for step_, *given in events.get(n, ()):
+            step_(*given)
+
+    def after_by_core(events, n):
+        if len(events) == 1 or events[0].get(n) == events[1].get(n):
+            return after(events[0], n)
+        for which in (0, 1):
+            if n in events[which]:
+                pl.when(core == which)(functools.partial(after, events[which], n))
+
+    def multiply(start, *events):
         n = 0
         for u in range(0, CH, 256):
             src, dst = pl.ds(u, 256), pl.ds(start + u, 256)
             for out, times in ((out_h, times_hh), (out_l, times_ll), (out_c, times_cross)):
                 out[dst, :] = times(a, b, src)
-                for step_, *given in events.get(n, ()):
-                    step_(*given)
+                after_by_core(events, n)
                 n += 1
 
-    multiply(
-        0,
+    def multiply_part(index, more, events):
+        start = pl.multiple_of(index * 256, 256)
+        n = 0
+        for u in range(0, CH, 256):
+            rows = pl.ds(u, 256)
+            for out, terms in (
+                (out_h, ((0, 1024),)),
+                (out_l, ((1024, 0),)),
+                (out_c, ((0, 0), (1024, 1024))),
+            ):
+                value = SCALE * sum(times_part(a, b, rows, start, *term) for term in terms)
+                out[rows, :] = out[rows, :] + value if more else value
+                after(events, n)
+                n += 1
+
+    multiply_part(x // 2, False, {1: ((right_third, 0), (right_third, 1))})
+    s4_send(1, 1, 2)
+    split_right(shard(2))
+    right_crossed(2, 9)
+    multiply_part(
+        1 - x // 2,
+        True,
         {
-            1: ((s4_send, 1, 1, 2),),
-            2: ((s4_send, 1, 3), (s3_send, 2, 1, 2, 3)),
+            1: ((s4_send, 1, 3), (s2_wait, 2), (s3_send, 2, 1, 2, 3)),
             3: ((s2_send, 3), (s3_send, 3, 0)),
         },
     )
@@ -268,10 +298,15 @@
             3: ((s2_wait, 3), (s3_send, 3, 3)),
             5: ((s4_send, 3, 0),),
         },
+        {2: ((s4_send, 2, 0, 1),), 3: ((s4_send, 2, 2, 3), (s2_wait, 3)), 4: ((s3_send, 3, 1),), 5: ((s3_send, 3, 2, 3),)},
     )
     s4_wait(2)
     collect(rl.at[2], a)
-    multiply(2 * CH, {0: ((s4_send, 3, 1),), 1: ((s4_send, 3, 2),), 2: ((s4_send, 3, 3),)})
+    multiply(
+        2 * CH,
+        {0: ((s4_send, 3, 1),), 1: ((s4_send, 3, 2),), 2: ((s4_send, 3, 3),)},
+        {1: ((s4_send, 3, 0, 1),), 2: ((s4_send, 3, 2),), 3: ((s4_send, 3, 3),)},
+    )
     s4_wait(3)
     arrived(rl.at[0, :, :, 0:3], near_sent.at[0])
     arrived(rl, far_sent.at[0])

time: 63.5 us -> 62.7 us (0.987)
  the two profiles are of different devices: /device:TPU:1 before, /device:TPU:0 now
where the time goes in v4:
time: 62.7 us; the launch traced here: 62.6 us
  Pallas kernels  61.8 us (99%)
  between operations  0.8 us (1%)
    pallas_call x1, Pallas kernels, per_device(): pl.pallas_call(gather_kernel, out_shape=[pltpu.VMEM((EARLY, N), F32)] * 3...  53.2 us
    pallas_call x1, Pallas kernels, per_device(): pl.pallas_call(finish_kernel, out_shape=[jax.ShapeDtypeStruct((M, N), F32...  8.51 us

profile of v4, /device:TPU:0, one launch (start us, length us, event | category | flops | bytes accessed | tf_op | source)
XLA Modules:
  0.0 62.6 jit_solution(4361748643099911033)
XLA Ops:
  0.6 53.2 %gather_multiply.1 = (f32[1536,1024]{1,0:T(8,128)S(1)}, f32[1536,1024]{1,0:T(8,128)S(1)}, f32[1536,1024]{1,0:T(8,128)S(1)}, f32[2,4,4,128,128]{4,3,2,1,0:T(8,128)S(1)}, bf16[2048,1024]{1,0:T(8,128)(2,1)S(1)}) custom-call(f32[32,2048]{1,0:T(8,128)} %bitcast.2, f32[32,2048]{1,0:T(8,128)} %bitcast.3, f32[64,1024]{1,0:T(8,128)} %rth.1, f32[64,1024]{1,0:T(8,128)} %rtl.1), custom_call_target="tpu_custom_call" | custom-call | flops 19327352832 | bytes 2097152 | tf_op jit(solution)/shard_map/gather_multiply/pallas_call | solution.py:341
  53.9 8.5 %multiply_write.1 = (f32[2048,1024]{1,0:T(8,128)}, f32[2048,1024]{1,0:T(8,128)}, f32[2048,1024]{1,0:T(8,128)}) custom-call(f32[1536,1024]{1,0:T(8,128)S(1)} %get-tuple-element.8.c_in, f32[1536,1024]{1,0:T(8,128)S(1)} %get-tuple-element.9.h_in, f32[1536,1024]{1,0:T(8,128)S(1)} %get-tuple-element.10.l_in, f32[2,4,4,128,128]{4,3,2,1,0:T(8,128)S(1)} %get-tuple-element.11.tiles, ...), custom_call_target="tpu_custom_call" | custom-call | flops 6442450944 | bytes 25165824 | tf_op jit(solution)/shard_map/multiply_write/pallas_call | solution.py:361

commit v5 on v4

--- a/solution.py
+++ b/solution.py
@@ -91,15 +91,14 @@
     xs = tuple(at(dx=d) for d in step)
     twin = at(dc=1)
 
-    loads = [pltpu.make_async_copy(ref, lt.at[i], load_sem.at[i]) for i, ref in enumerate((lth, ltl))]
-    own_right = [pltpu.make_async_copy(ref, rr.at[i, row], load_sem.at[2 + i]) for i, ref in enumerate((rth, rtl))]
-    for copy in loads + own_right:
-        copy.start()
     barrier = pltpu.get_barrier_semaphore()
     for device in (*yz[0], *yz[1], *xs, twin):
         pl.semaphore_signal(barrier, 1, device_id=device, device_id_type=MESH)
-    for copy in loads:
-        copy.wait()
+    for i, ref in enumerate((lth, ltl)):
+        pltpu.make_async_copy(ref, lt.at[i], load_sem.at[0]).start()
+    for i, ref in enumerate((rth, rtl)):
+        pltpu.make_async_copy(ref, rr.at[i, row], load_sem.at[1]).start()
+    pltpu.make_async_copy(lt, lt, load_sem.at[0]).wait()
 
     def chunk(c):
         return rl_last if c == NCH - 1 else rl.at[c]
@@ -209,8 +208,7 @@
     s1_send(1)
     pack(2)
     pack(3)
-    for copy in own_right:
-        copy.wait()
+    arrived(rr.at[:, row], load_sem.at[1])
     split_right(row)
     s2_send(0)
     s3_send(0, 1, 2)
@@ -313,26 +311,20 @@
     arrived(rr.at[:, 0:7], right_sent.at[0])
 
 
-def finish_kernel(c_in, h_in, l_in, tiles, b, c_out, h_out, l_out, a, stage, early_sem, late_sem):
-    copies = []
+def finish_kernel(c_in, h_in, l_in, tiles, b, c_out, h_out, l_out, a, stage, sem):
     for i, (src, dst) in enumerate(((c_in, c_out), (h_in, h_out), (l_in, l_out))):
-        for q, start in enumerate(range(0, EARLY, CH)):
-            rows = pl.ds(start, min(CH, EARLY - start))
-            copies.append(pltpu.make_async_copy(src.at[rows], dst.at[rows], early_sem.at[i, q]))
-            copies[-1].start()
+        for start in range(0, EARLY, CH):
+            rows = pl.ds(start, CH)
+            pltpu.make_async_copy(src.at[rows], dst.at[rows], sem.at[i]).start()
     collect(tiles, a)
     for u in range(2):
         rows = pl.ds(u * (LATE // 2), LATE // 2)
         for i, (times, dst) in enumerate(((times_cross, c_out), (times_hh, h_out), (times_ll, l_out))):
             stage[i, rows] = times(a, b, rows)
-            copies.append(
-                pltpu.make_async_copy(
-                    stage.at[i, rows], dst.at[pl.ds(EARLY + u * (LATE // 2), LATE // 2)], late_sem.at[i, u]
-                )
-            )
-            copies[-1].start()
-    for copy in copies:
-        copy.wait()
+            here = pl.ds(EARLY + u * (LATE // 2), LATE // 2)
+            pltpu.make_async_copy(stage.at[i, rows], dst.at[here], sem.at[i]).start()
+    for i, dst in enumerate((c_out, h_out, l_out)):
+        pltpu.make_async_copy(dst, dst, sem.at[i]).wait()
 
 
 def per_device(left_h, left_l, right_h, right_l):
@@ -349,7 +341,7 @@
             pltpu.VMEM((NCH - 1, 2, 4, 4, SUB, 128), F32),
             pltpu.VMEM((2, 8, RD, N), F32),
             pltpu.VMEM((CH, 4 * KW), BF16),
-            dma((4,)),
+            dma((2,)),
             dma((1,)), dma((1,)), dma((1,)), dma((NCH,)), dma((NCH,)), dma((NCH, 4)), dma((NCH,)), dma((10,)),
         ],
         compiler_params=pltpu.CompilerParams(
@@ -363,7 +355,7 @@
         out_shape=[jax.ShapeDtypeStruct((M, N), F32)] * 3,
         in_specs=[vmem] * 5,
         out_specs=[hbm] * 3,
-        scratch_shapes=[pltpu.VMEM((LATE, 4 * KW), BF16), pltpu.VMEM((3, LATE, N), F32), dma((3, 3)), dma((3, 2))],
+        scratch_shapes=[pltpu.VMEM((LATE, 4 * KW), BF16), pltpu.VMEM((3, LATE, N), F32), dma((3,))],
         compiler_params=pltpu.CompilerParams(vmem_limit_bytes=12 << 20),
         cost_estimate=pl.CostEstimate(flops=24 * LATE * N * KW, bytes_accessed=24 << 20, transcendentals=0),
         name="multiply_write",

time: 62.7 us -> 62.5 us (level)
  no operation moved by 1% of the time
where the time goes in v5:
time: 62.5 us; the launch traced here: 62.4 us
  Pallas kernels  61.6 us (99%)
  between operations  0.8 us (1%)
    pallas_call x1, Pallas kernels, per_device(): pl.pallas_call(gather_kernel, out_shape=[pltpu.VMEM((EARLY, N), F32)] * 3...  53.2 us
    pallas_call x1, Pallas kernels, per_device(): pl.pallas_call(finish_kernel, out_shape=[jax.ShapeDtypeStruct((M, N), F32...  8.4 us

profile of v5, /device:TPU:0, one launch (start us, length us, event | category | flops | bytes accessed | tf_op | source)
XLA Modules:
  0.0 62.4 jit_solution(8971796420788405032)
XLA Ops:
  0.6 53.2 %gather_multiply.1 = (f32[1536,1024]{1,0:T(8,128)S(1)}, f32[1536,1024]{1,0:T(8,128)S(1)}, f32[1536,1024]{1,0:T(8,128)S(1)}, f32[2,4,4,128,128]{4,3,2,1,0:T(8,128)S(1)}, bf16[2048,1024]{1,0:T(8,128)(2,1)S(1)}) custom-call(f32[32,2048]{1,0:T(8,128)} %bitcast.2, f32[32,2048]{1,0:T(8,128)} %bitcast.3, f32[64,1024]{1,0:T(8,128)} %rth.1, f32[64,1024]{1,0:T(8,128)} %rtl.1), custom_call_target="tpu_custom_call" | custom-call | flops 19327352832 | bytes 2097152 | tf_op jit(solution)/shard_map/gather_multiply/pallas_call | solution.py:333
  53.9 8.4 %multiply_write.1 = (f32[2048,1024]{1,0:T(8,128)}, f32[2048,1024]{1,0:T(8,128)}, f32[2048,1024]{1,0:T(8,128)}) custom-call(f32[1536,1024]{1,0:T(8,128)S(1)} %get-tuple-element.8.c_in, f32[1536,1024]{1,0:T(8,128)S(1)} %get-tuple-element.9.h_in, f32[1536,1024]{1,0:T(8,128)S(1)} %get-tuple-element.10.l_in, f32[2,4,4,128,128]{4,3,2,1,0:T(8,128)S(1)} %get-tuple-element.11.tiles, ...), custom_call_target="tpu_custom_call" | custom-call | flops 6442450944 | bytes 25165824 | tf_op jit(solution)/shard_map/multiply_write/pallas_call | solution.py:353

commit v6 on v5

--- a/solution.py
+++ b/solution.py
@@ -16,7 +16,7 @@
 CH = 512
 NCH = M // CH
 SUB = CH // 4
-BLK = 32
+BLK = 16
 LATE = CH
 EARLY = M - LATE
 

time: 62.5 us -> 62.5 us (level)
  no operation moved by 1% of the time
where the time goes in v6:
time: 62.5 us; the launch traced here: 62.3 us
  Pallas kernels  61.5 us (98%)
  between operations  0.8 us (1%)
    pallas_call x1, Pallas kernels, per_device(): pl.pallas_call(gather_kernel, out_shape=[pltpu.VMEM((EARLY, N), F32)] * 3...  53.2 us
    pallas_call x1, Pallas kernels, per_device(): pl.pallas_call(finish_kernel, out_shape=[jax.ShapeDtypeStruct((M, N), F32...  8.37 us

profile of v6, /device:TPU:0, one launch (start us, length us, event | category | flops | bytes accessed | tf_op | source)
XLA Modules:
  0.0 62.3 jit_solution(17449045699618786497)
XLA Ops:
  0.6 53.2 %gather_multiply.1 = (f32[1536,1024]{1,0:T(8,128)S(1)}, f32[1536,1024]{1,0:T(8,128)S(1)}, f32[1536,1024]{1,0:T(8,128)S(1)}, f32[2,4,4,128,128]{4,3,2,1,0:T(8,128)S(1)}, bf16[2048,1024]{1,0:T(8,128)(2,1)S(1)}) custom-call(f32[32,2048]{1,0:T(8,128)} %bitcast.2, f32[32,2048]{1,0:T(8,128)} %bitcast.3, f32[64,1024]{1,0:T(8,128)} %rth.1, f32[64,1024]{1,0:T(8,128)} %rtl.1), custom_call_target="tpu_custom_call" | custom-call | flops 19327352832 | bytes 2097152 | tf_op jit(solution)/shard_map/gather_multiply/pallas_call | solution.py:333
  53.8 8.4 %multiply_write.1 = (f32[2048,1024]{1,0:T(8,128)}, f32[2048,1024]{1,0:T(8,128)}, f32[2048,1024]{1,0:T(8,128)}) custom-call(f32[1536,1024]{1,0:T(8,128)S(1)} %get-tuple-element.8.c_in, f32[1536,1024]{1,0:T(8,128)S(1)} %get-tuple-element.9.h_in, f32[1536,1024]{1,0:T(8,128)S(1)} %get-tuple-element.10.l_in, f32[2,4,4,128,128]{4,3,2,1,0:T(8,128)S(1)} %get-tuple-element.11.tiles, ...), custom_call_target="tpu_custom_call" | custom-call | flops 6442450944 | bytes 25165824 | tf_op jit(solution)/shard_map/multiply_write/pallas_call | solution.py:353
